TPU v7x, 256 devices: a whole 4x4x8 slice. The times are simulated.
256 devices in a mesh: section: 2 (over core), wide: 16 (over y, z_lo), narrow: 8 (over z_hi, x).
Axes of the slice: x: 4, y: 4, z: 8 (z_hi: 2, z_lo: 4; z = z_hi * 4 + z_lo), core: 2. Of those that a mesh axis runs over, the one named last changes fastest.
Arguments:
- section_input: bfloat16 [2, 16, 14, 14, 2560], P('section', 'narrow', None, None, 'wide'), may hold values from -6 to 6
- kernels: bfloat16 [2, 3, 3, 2560, 2560], P('section', None, None, 'wide', 'narrow'), may hold values from -0.0390625 to 0.0390625
Outputs:
- section_out: bfloat16 [2, 16, 14, 14, 2560], P('section', 'narrow', None, None, 'wide')
- kernel_grads: float32 [2, 3, 3, 2560, 2560], P('section', None, None, 'wide', 'narrow')
All inputs are finite; a program needn't handle non-finite values.
Results may differ from a plain program's by a relative error of at most 0.0054.
Values may be sent and summed in bfloat16 or wider, within the bound.
A program may use at most 64 MiB of HBM per device.

v0:
```python
import math

import jax
import jax.numpy as jnp
from jax import lax
from jax.sharding import PartitionSpec as P


def from_partner(value, axis, distance):
    mask = 2**distance
    pairs = [(source, source ^ mask) for source in range(lax.axis_size(axis))]
    return lax.ppermute(value, axis, pairs)


def smooth(values):
    return values * jax.nn.sigmoid(values)


def smooth_slope(values):
    logistic = jax.nn.sigmoid(values)
    return logistic * (1.0 + values * (1.0 - logistic))


def spatial_conv(values, kernel, layout):
    return lax.conv_general_dilated(
        values,
        kernel,
        (1, 1),
        ((1, 1), (1, 1)),
        dimension_numbers=("NHWC", layout, "NHWC"),
        preferred_element_type=jnp.float32,
    )


def tap_sums(values, partner):
    return lax.conv_general_dilated(
        values,
        partner,
        (1, 1),
        ((1, 1), (1, 1)),
        dimension_numbers=("CHWN", "IHWO", "HWNC"),
        preferred_element_type=jnp.float32,
    )


def body(section_input, kernels):
    first_section = lax.axis_index("section") == 0
    kernel = kernels[0]
    turned = kernel[::-1, ::-1]
    forward_kernel = jnp.where(first_section, kernel, turned)
    backward_kernel = jnp.where(first_section, turned, kernel)
    gathered = lax.all_gather(section_input[0], "narrow", axis=0, tiled=True)
    images = gathered.shape[0]
    extent = gathered.shape[1]
    summed = lax.psum(spatial_conv(gathered, forward_kernel, "HWIO"), "wide")
    outgoing = jnp.where(first_section, smooth(summed), summed).astype(jnp.bfloat16)
    incoming = from_partner(outgoing, "section", 0).astype(jnp.float32)
    received = jnp.where(first_section, incoming * smooth_slope(summed), incoming).astype(
        jnp.bfloat16
    )
    row_count = images // lax.axis_size("narrow")
    image_block = lax.slice_in_dim(received, 0, row_count * lax.axis_size("narrow"), axis=0)
    result = lax.psum_scatter(
        spatial_conv(image_block, backward_kernel, "HWOI"),
        "narrow",
        scatter_dimension=0,
        tiled=True,
    ).astype(jnp.bfloat16)
    tap_grads = tap_sums(gathered, received) * (1.0 / math.sqrt(images * extent * extent))
    kernel_grads = jnp.where(first_section, tap_grads, tap_grads[::-1, ::-1])
    return (result[None], kernel_grads[None])


def solution(mesh):
    return jax.shard_map(
        body,
        mesh=mesh,
        in_specs=(
            P("section", "narrow", None, None, "wide"),
            P("section", None, None, "wide", "narrow"),
        ),
        out_specs=(
            P("section", "narrow", None, None, "wide"),
            P("section", None, None, "wide", "narrow"),
        ),
        check_vma=False,
    )
```

profile of v0, /device:TPU:2, one launch (start us, length us, event | category | flops | bytes accessed | tf_op | source)
XLA Modules:
  0.0 484.2 jit_solution(7891964328973895238)
XLA Ops:
  7.2 0.0 copy-start.2
  7.2 0.0 all-reduce.4.cloned.1.call-start
  7.2 1.0 copy.4
  8.3 57.1 %all-gather = bf16[1,16,14,14,160]{4,3,2,0,1:T(8,128)(2,1)S(1)} all-gather(bf16[1,2,14,14,160]{4,3,2,0,1:T(8,128)(2,1)S(1)} %copy.4), channel_id=2, replica_groups=mesh['section'=2,'wide'=16,'narrow'=8] {'narrow'}, dimensions={1}, use_global_device_ids=true | all-gather | bytes 1128960 | tf_op jit(solution)/shard_map/all_gather | solution.py:52
  65.3 0.0 copy-start
  65.3 0.0 copy-done.2
  65.3 1.5 reverse_select_fusion
  66.8 7.5 %fusion.4 = f32[16,14,14,320]{3,0,2,1:T(8,128)} fusion(bf16[3,3,160,320]{3,2,1,0:T(8,128)(2,1)S(1)} %get-tuple-element.3, bf16[1,16,14,14,160]{4,3,2,0,1:T(8,128)(2,1)S(1)} %all-gather), kind=kOutput, calls=%fused_computation.10 | convolution fusion | flops 2621440000 | bytes 5939200 | tf_op jit(solution)/shard_map/conv_general_dilated | solution.py:25
  74.3 0.0 copy-done
  74.3 0.0 all-reduce.4.cloned.1.call-update
  74.3 0.0 copy-start.4
  74.3 229.6 %all-reduce.4.cloned.1.call-done = f32[16,14,14,320]{3,0,2,1:T(8,128)} async-done(((f32[16,14,14,320]{3,0,2,1:T(8,128)}), f32[16,14,14,320]{3,0,2,1:T(8,128)}) %all-reduce.4.cloned.1.call-update) | async-done | bytes 4014096 | tf_op jit(solution)/shard_map/psum | solution.py:55
  303.9 3.7 fusion
  307.6 0.1 collective-permute-start
  307.7 0.0 copy-done.4
  307.7 0.6 dynamic-slice
  308.9 0.0 copy-start.1
  309.0 3.5 collective-permute-done
  312.4 4.3 fusion.1
  316.7 0.0 copy-done.1
  316.7 0.0 copy-start.3
  316.7 6.8 %fusion.2 = f32[3,3,160,320]{3,2,1,0:T(8,128)} fusion(bf16[16,14,14,320]{3,0,2,1:T(8,128)(2,1)S(1)} %fusion.1, bf16[1,16,14,14,160]{4,3,2,0,1:T(8,128)(2,1)S(1)} %copy-done.1), kind=kOutput, calls=%fused_computation.8 | convolution fusion | flops 2621440000 | bytes 4853760 | tf_op jit(solution)/shard_map/conv_general_dilated | solution.py:36
  323.5 0.0 copy-done.3
  323.5 6.3 %fusion.9 = f32[16,14,14,160]{3,0,2,1:T(8,128)S(1)} fusion(bf16[16,14,14,320]{3,0,2,1:T(8,128)(2,1)S(1)} %fusion.1, bf16[3,3,160,320]{3,2,1,0:T(8,128)(2,1)S(1)} %copy-done.3), kind=kOutput, calls=%fused_computation.16 | convolution fusion | flops 2621440000 | bytes 4935680 | tf_op jit(solution)/shard_map/conv_general_dilated | solution.py:25
  329.8 141.5 %all-reduce.5 = bf16[16,14,14,160]{3,0,2,1:T(8,128)(2,1)} all-reduce(f32[16,14,14,160]{3,0,2,1:T(8,128)S(1)} %fusion.9), channel_id=3, replica_groups=mesh['section'=2,'wide'=16,'narrow'=8] {'narrow'}, use_global_device_ids=true, to_apply=%region_1.2.clone | all-reduce | flops 501760 | bytes 3010560
  471.3 4.0 select_bitcast_fusion
  475.3 2.0 fusion.8
Async XLA Ops:
  7.2 58.2 %copy-start.2 = (bf16[1,3,3,160,320]{4,3,2,1,0:T(8,128)(2,1)S(1)}, bf16[1,3,3,160,320]{4,3,2,1,0:T(8,128)(2,1)}, u32[]{:S(2)}) copy-start(bf16[1,3,3,160,320]{4,3,2,1,0:T(8,128)(2,1)} %param.3) | copy-start | bytes 2764804
  7.2 296.7 %all-reduce.4.cloned.1.call-start = ((), (), s32[]{:S(2)}) async-start(), calls=%async_computation | async-start | bytes 9633792 | tf_op jit(solution)/shard_map/psum | solution.py:55
  65.3 9.0 %copy-start = (bf16[1,16,14,14,160]{4,3,2,0,1:T(8,128)(2,1)}, bf16[1,16,14,14,160]{4,3,2,0,1:T(8,128)(2,1)S(1)}, u32[]{:S(2)}) copy-start(bf16[1,16,14,14,160]{4,3,2,0,1:T(8,128)(2,1)S(1)} %all-gather) | copy-start | bytes 3010564
  74.3 233.4 %copy-start.4 = (u32[256]{0:T(256)S(1)}, u32[256]{0:T(256)}, u32[]{:S(2)}) copy-start(u32[256]{0:T(256)} %constant.16) | copy-start | bytes 3076
  307.6 4.8 collective-permute-start
  308.9 7.7 %copy-start.1 = (bf16[1,16,14,14,160]{4,3,2,0,1:T(8,128)(2,1)S(1)}, bf16[1,16,14,14,160]{4,3,2,0,1:T(8,128)(2,1)}, u32[]{:S(2)}) copy-start(bf16[1,16,14,14,160]{4,3,2,0,1:T(8,128)(2,1)} %copy-done) | copy-start | bytes 3010564
  316.7 6.8 %copy-start.3 = (bf16[3,3,160,320]{3,2,1,0:T(8,128)(2,1)S(1)}, bf16[3,3,160,320]{3,2,1,0:T(8,128)(2,1)}, u32[]{:S(2)}) copy-start(bf16[3,3,160,320]{3,2,1,0:T(8,128)(2,1)} %get-tuple-element.2) | copy-start | bytes 2764804
Sparse Core Ops, SparseCore 0:
  74.4 229.4 all-reduce.3
where the time goes:
time: 493 us; the launch traced here: 484 us
  waiting for transfers between devices  233 us (47%)
  blocking collectives  199 us (40%)
  matrix products  20.6 us (4%)
  between operations  14.8 us (3%)
  other arithmetic  13.4 us (3%)
    psum x1, waiting for transfers between devices, body(): summed = lax.psum(spatial_conv(gathered, forward_kernel, 'HWIO'), 'wide')  230 us
    unnamed x1, blocking collectives  141 us
    all_gather x1, blocking collectives, body(): gathered = lax.all_gather(section_input[0], 'narrow', axis=0, tiled=True)  57.1 us
    conv_general_dilated x2, matrix products, spatial_conv(): lax.conv_general_dilated(values, kernel, (1, 1), ((1, 1), (1, 1)), dimens...  13.8 us
  transfers between devices with their start and end apart: 2, of which 2 were waited for; matrix products, arithmetic and copies ran while one was open for 0% of the time, Pallas kernels for 0%

commit v1 on v0

v1 whole, which is shorter than its diff:
```python
import functools
import math

import jax
import jax.numpy as jnp
from jax import lax
from jax.experimental import pallas as pl
from jax.experimental.pallas import tpu as pltpu
from jax.sharding import PartitionSpec as P

MESH = pl.DeviceIdType.MESH

SIDE = 14
LANES = 512
CHUNKS = 8
TAPS = 9
BF16 = jnp.bfloat16
F32 = jnp.float32

SLOT = {(0, 0): 0, (0, 1): 1, (1, 0): 2, (1, 1): 3, (1, 3): 4, (1, 2): 5, (0, 3): 6, (0, 2): 7}


def chunk_dz(k):
    return ((k + 2) // 4) % 2


def chunk_dx(k):
    low = k % 2
    return low + (k // 4) * (3 - 2 * low)


def silu(values):
    return values * jax.nn.sigmoid(values)


def silu_slope(values):
    logistic = jax.nn.sigmoid(values)
    return logistic * (1.0 + values * (1.0 - logistic))


def tap_offset(tap):
    return (tap // 3 - 1) * 16 + (tap % 3 - 1)


def kernel(
    scale,
    x_ref,
    k_ref,
    out_ref,
    grad_ref,
    wide_x,
    taps,
    flipped,
    part,
    part_f,
    got_y,
    quarter,
    quarter_f,
    got_z,
    pre,
    ex_out,
    ex_in,
    act,
    act_all,
    products,
    share,
    got_x,
    own_sum,
    pair_out,
    pair_in,
    s_img,
    r_img,
    s_y,
    r_y,
    s_z,
    r_z,
    s_ex,
    r_ex,
    s_az,
    r_az,
    s_ay,
    r_ay,
    s_share,
    r_share,
    s_pair,
    r_pair,
):
    section = lax.axis_index("section")
    wide = lax.axis_index("wide")
    narrow = lax.axis_index("narrow")
    y, zl = wide // 4, wide % 4
    zh, x = narrow // 4, narrow % 4

    def at_y(j):
        return (section, ((y + j) % 4) * 4 + zl, narrow)

    def at_z(j):
        return (section, y * 4 + (zl + j) % 4, narrow)

    def at_x(j):
        return (section, wide, zh * 4 + (x + j) % 4)

    pair = (section, wide, (1 - zh) * 4 + x)
    other = (1 - section, wide, narrow)

    def copy(src, dst, send, recv, device):
        return pltpu.make_async_remote_copy(
            src_ref=src, dst_ref=dst, send_sem=send, recv_sem=recv, device_id=device, device_id_type=MESH
        )

    barrier = pltpu.get_barrier_semaphore()
    peers = [at_y(j) for j in (1, 2, 3)] + [at_z(j) for j in (1, 2, 3)]
    peers += [at_x(j) for j in (1, 2, 3)] + [pair, other]
    for peer in peers:
        pl.semaphore_signal(barrier, inc=1, device_id=peer, device_id_type=MESH)

    blank = jnp.zeros((SIDE, 2, x_ref.shape[2]), BF16)
    rows = []
    for image in range(2):
        tile = x_ref[image * SIDE : (image + 1) * SIDE]
        tile = jnp.concatenate([tile, blank], axis=1)
        rows.append(tile.reshape(SIDE * 16, x_ref.shape[2]))
        rows.append(jnp.zeros((32, x_ref.shape[2]), BF16))
    wide_x[0] = jnp.concatenate(rows, axis=0).T

    pl.semaphore_wait(barrier, len(peers))

    def image_copy(slot, dz, j):
        there = SLOT[(dz, (4 - j) % 4)]
        return copy(wide_x.at[slot], wide_x.at[there], s_img.at[there], r_img.at[there], at_x(j))

    to_pair = copy(wide_x.at[0], wide_x.at[2], s_img.at[2], r_img.at[2], pair)
    to_pair.start()
    image_copy(0, 0, 3).start()

    flipped[...] = k_ref[...].T
    grad_ref[...] = jnp.zeros_like(grad_ref)

    sign = 1 - 2 * section
    lane = lax.broadcasted_iota(jnp.int32, (1, 128), 1)
    row = (zl % 2) * 8 + lane // 16
    inside = ((lane % 16 < SIDE) & (row < SIDE)).astype(F32)

    def shift_of(tap, direction):
        return (LANES - direction * tap_offset(tap)) % LANES

    def y_copy(k, j):
        return copy(
            part.at[k, (y + j) % 4], got_y.at[k, j - 1], s_y.at[k, j - 1], r_y.at[k, j - 1], at_y(j)
        )

    def z_copy(k, j):
        return copy(
            quarter.at[k, (zl + j) % 4], got_z.at[k, j - 1], s_z.at[k, j - 1], r_z.at[k, j - 1], at_z(j)
        )

    def ex_copy(k):
        return copy(ex_out.at[k], ex_in.at[k], s_ex.at[k], r_ex.at[k], other)

    def az_copy(k, j):
        here = act.at[k, y, zl]
        return copy(here, here, s_az.at[k, j - 1], r_az.at[k, j - 1], at_z(j))

    def ay_copy(k, j):
        here = act.at[k, y]
        return copy(here, here, s_ay.at[k, j - 1], r_ay.at[k, j - 1], at_y(j))

    def share_copy(k):
        dz, dx = chunk_dz(k), chunk_dx(k)
        slot = 3 - dx
        return copy(share.at[k], got_x.at[dz, slot], s_share.at[k], r_share.at[dz, slot], at_x(dx))

    def arrived(buffer, send, recv, device):
        copy(buffer, buffer, send, recv, device).wait_recv()

    def first_conv(k):
        @pl.when((k > 0) & (k != 2))
        def _():
            arrived(wide_x.at[k], s_img.at[k], r_img.at[k], pair)

        image = wide_x[k]
        for tap in range(TAPS):
            moved = image if tap == 4 else pltpu.roll(image, shift_of(tap, sign), 1)
            taps[k, pl.ds(160 * tap, 160), :] = moved
        total = jnp.dot(flipped[...], taps[k], preferred_element_type=F32)
        for block in range(4):
            piece = total[80 * block : 80 * block + 80]
            part_f[k % 2, block] = piece
            part[k, block] = piece.astype(BF16)
        for j in (1, 3, 2):
            y_copy(k, j).start()

    def sum_y(k):
        for j in (1, 2, 3):
            arrived(got_y.at[k, j - 1], s_y.at[k, j - 1], r_y.at[k, j - 1], at_y(j))
        total = part_f[k % 2, y]
        for j in range(3):
            total = total + got_y[k, j].astype(F32)
        for block in range(4):
            piece = total[:, 128 * block : 128 * block + 128]
            quarter_f[k % 2, block] = piece
            quarter[k, block] = piece.astype(BF16)
        for j in (1, 2, 3):
            z_copy(k, j).start()

    def sum_z(k):
        for j in (1, 2, 3):
            arrived(got_z.at[k, j - 1], s_z.at[k, j - 1], r_z.at[k, j - 1], at_z(j))
        total = quarter_f[k % 2, zl]
        for j in range(3):
            total = total + got_z[k, j].astype(F32)
        pre[k] = total
        sent = jnp.where(section == 0, silu(total), total) * inside
        ex_out[k] = sent.astype(BF16)
        ex_copy(k).start()

    def meet(k):
        arrived(ex_in.at[k], s_ex.at[k], r_ex.at[k], other)
        incoming = ex_in[k].astype(F32)
        received = jnp.where(section == 0, incoming * silu_slope(pre[k]), incoming)
        act[k, y, zl] = received.astype(BF16)
        for j in (1, 2, 3):
            az_copy(k, j).start()

    def spread_y(k):
        for j in (1, 2, 3):
            arrived(act.at[k, y, (zl + j) % 4], s_az.at[k, j - 1], r_az.at[k, 3 - j], at_z(j))
        for j in (1, 3, 2):
            ay_copy(k, j).start()

    def second_conv(k):
        for j in (1, 2, 3):
            arrived(act.at[k, (y + j) % 4], s_ay.at[k, j - 1], r_ay.at[k, 3 - j], at_y(j))
        for a in range(4):
            for b in range(4):
                act_all[pl.ds(80 * a, 80), pl.ds(128 * b, 128)] = act[k, a, b]
        products[...] = jnp.dot(k_ref[...], act_all[...], preferred_element_type=F32)
        total = products[pl.ds(160 * 4, 160), :]
        for tap in range(TAPS):
            if tap != 4:
                moved = pltpu.roll(products[pl.ds(160 * tap, 160), :], shift_of(tap, -sign), 1)
                total = total + moved
        dx = chunk_dx(k)

        @pl.when(dx == 0)
        def _():
            own_sum[chunk_dz(k)] = total

        @pl.when(dx != 0)
        def _():
            share[k] = total.astype(BF16)
            share_copy(k).start()

        grad_ref[...] += lax.dot_general(
            taps[k], act_all[...], (((1,), (1,)), ((), ())), preferred_element_type=F32
        )

    def sum_x(dz):
        total = own_sum[dz]
        for j in range(3):
            arrived(got_x.at[dz, j], s_share.at[1], r_share.at[dz, j], at_x(1))
            total = total + got_x[dz, j].astype(F32)
        return total

    def step(t, carry):
        @pl.when(t < CHUNKS)
        def _():
            first_conv(t)

        @pl.when(t == 0)
        def _():
            image_copy(0, 0, 1).start()
            image_copy(0, 0, 2).start()

        @pl.when(t == 1)
        def _():
            arrived(wide_x.at[2], s_img.at[2], r_img.at[2], pair)
            for j in (3, 1, 2):
                image_copy(2, 1, j).start()

        for lag, stage in ((4, spread_y), (3, meet), (2, sum_z), (1, sum_y), (5, second_conv)):

            @pl.when((t >= lag) & (t < CHUNKS + lag))
            def _():
                stage(t - lag)

        return carry

    lax.fori_loop(0, CHUNKS + 5, step, 0)

    pair_out[...] = sum_x(1).astype(BF16)
    across = copy(pair_out, pair_in, s_pair, r_pair, pair)
    across.start()
    grad_ref[...] *= scale
    total = sum_x(0)
    across.wait_recv()
    total = (total + pair_in[...].astype(F32)).astype(BF16)
    turned = total.T.reshape(LANES // 16, 16, out_ref.shape[2])
    for image in range(2):
        out_ref[image * SIDE : (image + 1) * SIDE] = turned[16 * image : 16 * image + SIDE, :SIDE]

    across.wait_send()
    to_pair.wait_send()
    for j in (1, 2, 3):
        image_copy(0, 0, j).wait_send()
        image_copy(2, 1, j).wait_send()

    def finish(k, carry):
        for j in (1, 2, 3):
            y_copy(k, j).wait_send()
            z_copy(k, j).wait_send()
            az_copy(k, j).wait_send()
            ay_copy(k, j).wait_send()
        ex_copy(k).wait_send()

        @pl.when(chunk_dx(k) != 0)
        def _():
            share_copy(k).wait_send()

        return carry

    lax.fori_loop(0, CHUNKS, finish, 0)


def body(section_input, kernels):
    images, channels = section_input.shape[1], section_input.shape[4]
    inner = kernels.shape[4]
    scale = 1.0 / math.sqrt(CHUNKS * images * SIDE * SIDE)
    sem = pltpu.SemaphoreType.DMA
    out, grads = pl.pallas_call(
        functools.partial(kernel, scale),
        out_shape=(
            jax.ShapeDtypeStruct((images * SIDE, SIDE, channels), BF16),
            jax.ShapeDtypeStruct((TAPS * channels, inner), F32),
        ),
        in_specs=[pl.BlockSpec(memory_space=pltpu.VMEM)] * 2,
        out_specs=[pl.BlockSpec(memory_space=pltpu.VMEM)] * 2,
        scratch_shapes=[
            pltpu.VMEM((CHUNKS, channels, LANES), BF16),
            pltpu.VMEM((CHUNKS, TAPS * channels, LANES), BF16),
            pltpu.VMEM((inner, TAPS * channels), BF16),
            pltpu.VMEM((CHUNKS, 4, 80, LANES), BF16),
            pltpu.VMEM((2, 4, 80, LANES), F32),
            pltpu.VMEM((CHUNKS, 3, 80, LANES), BF16),
            pltpu.VMEM((CHUNKS, 4, 80, 128), BF16),
            pltpu.VMEM((2, 4, 80, 128), F32),
            pltpu.VMEM((CHUNKS, 3, 80, 128), BF16),
            pltpu.VMEM((CHUNKS, 80, 128), F32),
            pltpu.VMEM((CHUNKS, 80, 128), BF16),
            pltpu.VMEM((CHUNKS, 80, 128), BF16),
            pltpu.VMEM((CHUNKS, 4, 4, 80, 128), BF16),
            pltpu.VMEM((inner, LANES), BF16),
            pltpu.VMEM((TAPS * channels, LANES), F32),
            pltpu.VMEM((CHUNKS, channels, LANES), BF16),
            pltpu.VMEM((2, 3, channels, LANES), BF16),
            pltpu.VMEM((2, channels, LANES), F32),
            pltpu.VMEM((channels, LANES), BF16),
            pltpu.VMEM((channels, LANES), BF16),
            sem((CHUNKS,)),
            sem((CHUNKS,)),
            sem((CHUNKS, 3)),
            sem((CHUNKS, 3)),
            sem((CHUNKS, 3)),
            sem((CHUNKS, 3)),
            sem((CHUNKS,)),
            sem((CHUNKS,)),
            sem((CHUNKS, 3)),
            sem((CHUNKS, 3)),
            sem((CHUNKS, 3)),
            sem((CHUNKS, 3)),
            sem((CHUNKS,)),
            sem((2, 3)),
            sem,
            sem,
        ],
        compiler_params=pltpu.CompilerParams(
            collective_id=0, has_side_effects=True, vmem_limit_bytes=60 * 2**20
        ),
        name="relay",
    )(
        section_input.reshape(images * SIDE, SIDE, channels),
        kernels.reshape(TAPS * channels, inner),
    )
    return (
        out.reshape(section_input.shape),
        grads.reshape(kernels.shape),
    )


def solution(mesh):
    return jax.shard_map(
        body,
        mesh=mesh,
        in_specs=(
            P("section", "narrow", None, None, "wide"),
            P("section", None, None, "wide", "narrow"),
        ),
        out_specs=(
            P("section", "narrow", None, None, "wide"),
            P("section", None, None, "wide", "narrow"),
        ),
        check_vma=False,
    )
```

time: 493 us -> 99.7 us (0.20); the launches traced: 484 us -> 99.5 us
  waiting for transfers between devices: 233 us -> 0 us
  blocking collectives: 199 us -> 0 us
  Pallas kernels: 0 us -> 92.2 us
  matrix products: 20.6 us -> 0 us
  between operations: 14.8 us -> 0.64 us
  other arithmetic: 13.4 us -> 0 us
    psum x1 -> x0, waiting for transfers between devices: 230 us -> none  [body(): summed = lax.psum(spatial_conv(gathered, forward_kernel, 'HWIO'), 'wide')]
    unnamed x1 -> x0, blocking collectives: 141 us -> none
    pallas_call x0 -> x1, Pallas kernels: none -> 92.2 us  [body(): pl.pallas_call(functools.partial(kernel, scale), out_shape=(jax.ShapeDtyp...]
    all_gather x1 -> x0, blocking collectives: 57.1 us -> none  [body(): gathered = lax.all_gather(section_input[0], 'narrow', axis=0, tiled=True)]
    conv_general_dilated x3 -> x0, matrix products: 20.6 us -> none  [the longest x2 13.8 us: spatial_conv(): lax.conv_general_dilated(values, kernel, (1, 1), ((1, 1), (1, 1)), dimens...]
    convert_element_type x2 -> x0, other arithmetic: 7.91 us -> none  [the longest x1 4.25 us: body(): jnp.where(first_section, incoming * smooth_slope(summed), incoming)]
    unnamed x12 -> x3, local copies, waits for them, and re-layouts: 1.65 us -> 6.59 us
  transfers between devices with their start and end apart: 2 -> 0, of which waited for: 2 -> 0; matrix products, arithmetic and copies ran while one was open for 0% -> 0% of each run, Pallas kernels for 0% -> 0%
where the time goes in v1:
time: 99.7 us; the launch traced here: 99.5 us
  Pallas kernels  92.2 us (92%)
  local copies, waits for them, and re-layouts  6.59 us (7%)
    pallas_call x1, Pallas kernels, body(): pl.pallas_call(functools.partial(kernel, scale), out_shape=(jax.ShapeDtyp...  92.2 us
    unnamed x3, local copies, waits for them, and re-layouts  6.59 us

profile of v1, /device:TPU:2, one launch (start us, length us, event | category | flops | bytes accessed | tf_op | source)
XLA Modules:
  0.0 99.5 jit_solution(6817400333481365911)
XLA Ops:
  0.6 1.6 %copy.4 = bf16[1,2,14,14,160]{4,3,2,1,0:T(8,128)(2,1)} copy(bf16[1,2,14,14,160]{4,1,3,2,0:T(2,128)(2,1)} %param.2) | data formatting | bytes 250880 | tf_op args[0]
  2.3 92.2 %relay.1 = (bf16[28,14,160]{2,1,0:T(8,128)(2,1)}, f32[1440,320]{1,0:T(8,128)}) custom-call(bf16[28,14,160]{2,1,0:T(8,128)(2,1)} %bitcast.6, bf16[1440,320]{1,0:T(8,128)(2,1)} %bitcast.5), custom_call_target="tpu_custom_call" | custom-call | tf_op jit(solution)/shard_map/relay/pallas_call | solution.py:330
  94.5 1.8 %copy.5 = bf16[1,2,14,14,160]{4,1,3,2,0:T(2,128)(2,1)} copy(bf16[1,2,14,14,160]{4,3,2,1,0:T(8,128)(2,1)} %bitcast.7) | data formatting | bytes 250880
  96.3 3.1 %copy.7 = f32[1,3,3,160,320]{4,3,2,1,0:T(8,128)} copy(f32[1,3,3,160,320]{4,3,2,1,0:T(8,128)} %bitcast.4) | data formatting | bytes 3686400

commit v2 on v0

v2 whole, which is shorter than its diff:
```python
import math

import jax
import jax.numpy as jnp
from jax import lax
from jax.experimental import pallas as pl
from jax.experimental.pallas import tpu as pltpu
from jax.sharding import PartitionSpec as P

MESH = pl.DeviceIdType.MESH
BF16 = jnp.bfloat16
F32 = jnp.float32

SIDE = 14
CHUNKS = 8
PIXELS = 2 * SIDE * SIDE
LANES = 512
SPILL = PIXELS - 384
TAPS = 9
ROWS_A = 160
ROWS_B = 320
BLOCK_A = 3 * ROWS_A + 16
BLOCK_B = 3 * (ROWS_B // 4) + 16
HALF = BLOCK_B // 2
QUARTER = BLOCK_B // 4

SLOT = {(0, 0): 0, (0, 1): 1, (0, 2): 2, (1, 0): 3, (1, 1): 4, (1, 2): 5, (1, 3): 6, (0, 3): 7}
FROM_PAIR = SLOT[(1, 0)]

PLAN = (
    (0, 1, "next_conv"),
    (1, 0, "join"),
    (5, 0, "spread_y"),
    (3, 0, "sum_z"),
    (6, 0, "forward_y"),
    (2, 0, "sum_y"),
    (7, 1, "second_conv"),
    (3, 0, "meet"),
    (9, 1, "kernel_grad"),
)
LAST = 7
LATE_GRADS = (6, 7, 0)


def chunk_dz(k):
    return ((k + 1) // 4) % 2


def chunk_dx(k):
    late = k // 6
    return (1 - late) * (k % 3) + 3 * late


def silu(values):
    return values * jax.nn.sigmoid(values)


def silu_slope(values):
    logistic = jax.nn.sigmoid(values)
    return logistic * (1.0 + values * (1.0 - logistic))


def pack(values):
    rows = values.shape[0]
    spilled = values[:16, 384:]
    for group in range(1, rows // 16):
        spilled = spilled + pltpu.roll(values[16 * group : 16 * group + 16, 384:], SPILL * group, 1)
    return jnp.concatenate([values[:, 0:128], values[:, 128:256], values[:, 256:384], spilled], axis=0)


def unpack(block, rows, keep):
    spilled = block[3 * rows :]
    last = [spilled * keep]
    for group in range(1, rows // 16):
        last.append(pltpu.roll(spilled, 128 - SPILL * group, 1) * keep)
    parts = [block[0:rows], block[rows : 2 * rows], block[2 * rows : 3 * rows], jnp.concatenate(last, axis=0)]
    return jnp.concatenate(parts, axis=1)


def kernel(
    x_ref,
    k_hbm,
    out_ref,
    grad_ref,
    k_ref,
    masks,
    masks_f,
    images,
    taps,
    flipped,
    part,
    part_f,
    relayed,
    joined,
    got_y,
    quarter,
    quarter_f,
    got_z,
    pre,
    ex_out,
    ex_in,
    act,
    act_all,
    products,
    share,
    got_x,
    own_sum,
    pair_out,
    pair_in,
    s_load,
    s_img,
    s_relay,
    s_near,
    s_join,
    s_z,
    s_ex,
    s_az,
    s_ay,
    s_af,
    s_share,
    s_pair,
    r_img,
    r_relay,
    r_y,
    r_z,
    r_ex,
    r_az,
    r_ay,
    r_af,
    r_share,
    r_pair,
):
    section = lax.axis_index("section")
    wide = lax.axis_index("wide")
    narrow = lax.axis_index("narrow")
    y, zl = wide // 4, wide % 4
    zh, x = narrow // 4, narrow % 4

    def at_y(j):
        return (section, ((y + j) % 4) * 4 + zl, narrow)

    def at_z(j):
        return (section, y * 4 + (zl + j) % 4, narrow)

    def at_x(j):
        return (section, wide, zh * 4 + (x + j) % 4)

    pair = (section, wide, (1 - zh) * 4 + x)
    other = (1 - section, wide, narrow)

    def copy(src, dst, send, recv, device):
        return pltpu.make_async_remote_copy(
            src_ref=src, dst_ref=dst, send_sem=send, recv_sem=recv, device_id=device, device_id_type=MESH
        )

    barrier = pltpu.get_barrier_semaphore()
    peers = [at_y(j) for j in (1, 3)] + [at_z(j) for j in (1, 2, 3)]
    peers += [at_x(j) for j in (1, 2, 3)] + [pair, other]
    for peer in peers:
        pl.semaphore_signal(barrier, inc=1, device_id=peer, device_id_type=MESH)

    load = pltpu.make_async_copy(k_hbm, k_ref, s_load)
    load.start()

    sign = 1 - 2 * section
    lane = lax.broadcasted_iota(jnp.int32, (1, LANES), 1)
    pixel = lane // 2
    row = pixel // SIDE
    column = pixel - SIDE * row
    for tap in range(TAPS):
        there_row = row + sign * (tap // 3 - 1)
        there_column = column + sign * (tap % 3 - 1)
        inside = (there_row >= 0) & (there_row < SIDE) & (there_column >= 0) & (there_column < SIDE)
        inside = (inside & (lane < PIXELS)).astype(F32)
        masks_f[tap] = inside
        masks[tap] = inside.astype(BF16)
    keep = (lane[:, :128] < SPILL).astype(BF16)

    def shift_of(tap, direction):
        offset = 2 * ((tap // 3 - 1) * SIDE + tap % 3 - 1)
        return (LANES - direction * offset) % LANES

    blank = jnp.zeros((LANES - PIXELS, ROWS_A), F32)
    own_f = jnp.concatenate([x_ref[...].astype(F32), blank], axis=0).T
    own = own_f.astype(BF16)
    images[0] = pack(own_f).astype(BF16)
    grad_ref[...] = jnp.zeros_like(grad_ref)

    def image_copy(slot, dz, j):
        there = SLOT[(dz, (4 - j) % 4)]
        return copy(images.at[slot], images.at[there], s_img, r_img.at[there], at_x(j))

    to_pair = copy(images.at[0], images.at[FROM_PAIR], s_img, r_img.at[FROM_PAIR], pair)

    def relay_copy(k, half):
        return copy(
            part.at[k, (y + 2) % 4, half], relayed.at[k, half], s_relay, r_relay.at[k], at_y(1 + 2 * half)
        )

    def near_copy(k, half):
        j = 3 - 2 * half
        return copy(part.at[k, (y + j) % 4, half], got_y.at[k, 0, half], s_near, r_y.at[k], at_y(j))

    def join_copy(k, half):
        return copy(joined.at[k, half], got_y.at[k, 1, half], s_join, r_y.at[k], at_y(1 + 2 * half))

    def z_copy(k, j):
        return copy(quarter.at[k, (zl + j) % 4], got_z.at[k, j - 1], s_z, r_z.at[k], at_z(j))

    def ex_copy(k):
        return copy(ex_out.at[k], ex_in.at[k], s_ex, r_ex.at[k], other)

    def az_copy(k, j):
        here = act.at[k, y, zl]
        return copy(here, here, s_az, r_az.at[k], at_z(j))

    def ay_copy(k, side):
        here = act.at[k, y]
        return copy(here, here, s_ay, r_ay.at[k], at_y(1 + 2 * side))

    def af_copy(k, side):
        here = act.at[k, (y + 3 - 2 * side) % 4, pl.ds(2 * side, 2)]
        return copy(here, here, s_af, r_af.at[k], at_y(1 + 2 * side))

    def share_copy(k):
        dz, dx = chunk_dz(k), chunk_dx(k)
        return copy(share.at[k], got_x.at[dz, 3 - dx], s_share, r_share.at[dz], at_x(dx))

    def arrived(buffer, recv):
        copy(buffer, buffer, s_pair, recv, other).wait_recv()

    def left(buffer, send):
        copy(buffer, buffer, send, r_pair, other).wait_send()

    def first_conv(k):
        image = own if isinstance(k, int) else unpack(images[k], ROWS_A, keep)
        for tap in range(TAPS):
            moved = image
            if tap != 4:
                moved = pltpu.roll(image, shift_of(tap, sign), 1) * masks[tap]
            taps[k, pl.ds(ROWS_A * tap, ROWS_A), :] = moved
        total = jnp.dot(flipped[...], taps[k], preferred_element_type=F32)
        for block in range(4):
            piece = pack(total[80 * block : 80 * block + 80])
            for half in range(2):
                rows = piece[HALF * half : HALF * half + HALF]
                part_f[k, block, half] = rows
                part[k, block, half] = rows.astype(BF16)

    def send_parts(k):
        for half in range(2):
            relay_copy(k, half).start()
        for half in range(2):
            near_copy(k, half).start()

    def next_conv(k):
        @pl.when(k != FROM_PAIR)
        def _():
            arrived(images.at[k], r_img.at[k])

        first_conv(k)
        send_parts(k)

    def join(k):
        arrived(relayed.at[k], r_relay.at[k])
        for half in range(2):
            total = part_f[k, (y + 1 + 2 * half) % 4, half] + relayed[k, half].astype(F32)
            joined[k, half] = total.astype(BF16)
            join_copy(k, half).start()

    def sum_y(k):
        arrived(got_y.at[k], r_y.at[k])
        for half in range(2):
            total = part_f[k, y, half]
            for j in range(2):
                total = total + got_y[k, j, half].astype(F32)
            for side in range(2):
                piece = total[QUARTER * side : QUARTER * side + QUARTER]
                quarter_f[k, 2 * half + side] = piece
                quarter[k, 2 * half + side] = piece.astype(BF16)
        for j in (2, 3, 1):
            z_copy(k, j).start()

    def sum_z(k):
        arrived(got_z.at[k], r_z.at[k])
        total = quarter_f[k, zl]
        for j in range(3):
            total = total + got_z[k, j].astype(F32)
        pre[k] = total
        ex_out[k] = jnp.where(section == 0, silu(total), total).astype(BF16)
        ex_copy(k).start()

    def meet(k):
        arrived(ex_in.at[k], r_ex.at[k])
        incoming = ex_in[k].astype(F32)
        received = jnp.where(section == 0, incoming * silu_slope(pre[k]), incoming)
        act[k, y, zl] = received.astype(BF16)
        for j in (2, 3, 1):
            az_copy(k, j).start()

    def spread_y(k):
        arrived(got_z.at[k], r_az.at[k])
        for side in range(2):
            ay_copy(k, side).start()

    def forward_y(k):
        arrived(act.at[k, pl.ds(0, 2)], r_ay.at[k])
        for side in range(2):
            af_copy(k, side).start()

    def second_conv(k):
        arrived(act.at[k, 0], r_af.at[k])
        for block in range(4):
            piece = unpack(act[k, block].reshape(BLOCK_B, 128), 80, keep)
            act_all[k, pl.ds(80 * block, 80), :] = piece
        products[...] = jnp.dot(k_ref[...], act_all[k], preferred_element_type=F32)
        total = products[pl.ds(ROWS_A * 4, ROWS_A), :]
        for tap in range(TAPS):
            if tap != 4:
                moved = pltpu.roll(products[pl.ds(ROWS_A * tap, ROWS_A), :], shift_of(tap, -sign), 1)
                total = total + moved * masks_f[8 - tap]
        block = pack(total)
        if isinstance(k, int):
            own_sum[0] = block
            return
        dx = chunk_dx(k)

        @pl.when(dx == 0)
        def _():
            own_sum[chunk_dz(k)] = block

        @pl.when(dx != 0)
        def _():
            share[k] = block.astype(BF16)
            share_copy(k).start()

    def kernel_grad(k):
        grad_ref[...] += lax.dot_general(
            taps[k], act_all[k], (((1,), (1,)), ((), ())), preferred_element_type=F32
        )

    def sum_x(dz):
        arrived(got_x.at[dz], r_share.at[dz])
        total = own_sum[dz]
        for j in range(3):
            total = total + got_x[dz, j].astype(F32)
        return total

    stages = dict(
        next_conv=next_conv,
        join=join,
        sum_y=sum_y,
        sum_z=sum_z,
        meet=meet,
        spread_y=spread_y,
        forward_y=forward_y,
        second_conv=second_conv,
        kernel_grad=kernel_grad,
    )

    def step(t, carry):
        for when, j in ((1, 2), (5, 1)):

            @pl.when(t == when)
            def _():
                image_copy(0, 0, j).start()

        @pl.when(t == FROM_PAIR)
        def _():
            arrived(images.at[FROM_PAIR], r_img.at[FROM_PAIR])
            for j in (3, 2, 1):
                image_copy(FROM_PAIR, 1, j).start()

        for lag, first, stage in PLAN:

            @pl.when((t >= lag + first) & (t < CHUNKS + lag))
            def _():
                stages[stage](t - lag)

        return carry

    load.wait()
    flipped[...] = k_ref[...].T
    first_conv(0)
    pl.semaphore_wait(barrier, len(peers))
    to_pair.start()
    image_copy(0, 0, 3).start()
    send_parts(0)

    lax.fori_loop(1, CHUNKS + LAST, step, 0)

    across = copy(pair_out, pair_in, s_pair, r_pair, pair)
    pair_out[...] = sum_x(1).astype(BF16)
    across.start()
    second_conv(0)
    for k in LATE_GRADS:
        kernel_grad(k)
    total = sum_x(0)
    across.wait_recv()
    total = total + pair_in[...].astype(F32)
    out_ref[...] = unpack(total, ROWS_A, keep.astype(F32)).T[:PIXELS].astype(BF16)

    across.wait_send()
    left(images.at[pl.ds(0, 7)], s_img)
    left(relayed, s_relay)
    left(relayed, s_near)
    left(relayed, s_join)
    left(got_z, s_z)
    left(ex_out, s_ex)
    left(got_z, s_az)
    left(act.at[:, pl.ds(0, 2)], s_ay)
    left(act.at[:, 0], s_af)
    left(share.at[pl.ds(0, 6)], s_share)


def body(section_input, kernels):
    images, channels = section_input.shape[1], section_input.shape[4]
    inner = kernels.shape[4]
    scale = 1.0 / math.sqrt(CHUNKS * images * SIDE * SIDE)
    sem = pltpu.SemaphoreType.DMA
    pixels_first = section_input[0].transpose(1, 2, 0, 3).reshape(PIXELS, channels)
    out, grads = pl.pallas_call(
        kernel,
        out_shape=(
            jax.ShapeDtypeStruct((PIXELS, channels), BF16),
            pltpu.VMEM((TAPS * channels, inner), F32),
        ),
        in_specs=[pl.BlockSpec(memory_space=pltpu.VMEM), pl.BlockSpec(memory_space=pl.ANY)],
        out_specs=[pl.BlockSpec(memory_space=pltpu.VMEM)] * 2,
        scratch_shapes=[
            pltpu.VMEM((TAPS * channels, inner), BF16),
            pltpu.VMEM((TAPS, 1, LANES), BF16),
            pltpu.VMEM((TAPS, 1, LANES), F32),
            pltpu.VMEM((CHUNKS, BLOCK_A, 128), BF16),
            pltpu.VMEM((CHUNKS, TAPS * channels, LANES), BF16),
            pltpu.VMEM((inner, TAPS * channels), BF16),
            pltpu.VMEM((CHUNKS, 4, 2, HALF, 128), BF16),
            pltpu.VMEM((CHUNKS, 4, 2, HALF, 128), F32),
            pltpu.VMEM((CHUNKS, 2, HALF, 128), BF16),
            pltpu.VMEM((CHUNKS, 2, HALF, 128), BF16),
            pltpu.VMEM((CHUNKS, 2, 2, HALF, 128), BF16),
            pltpu.VMEM((CHUNKS, 4, QUARTER, 128), BF16),
            pltpu.VMEM((CHUNKS, 4, QUARTER, 128), F32),
            pltpu.VMEM((CHUNKS, 3, QUARTER, 128), BF16),
            pltpu.VMEM((CHUNKS, QUARTER, 128), F32),
            pltpu.VMEM((CHUNKS, QUARTER, 128), BF16),
            pltpu.VMEM((CHUNKS, QUARTER, 128), BF16),
            pltpu.VMEM((CHUNKS, 4, 4, QUARTER, 128), BF16),
            pltpu.VMEM((CHUNKS, inner, LANES), BF16),
            pltpu.VMEM((TAPS * channels, LANES), F32),
            pltpu.VMEM((CHUNKS, BLOCK_A, 128), BF16),
            pltpu.VMEM((2, 3, BLOCK_A, 128), BF16),
            pltpu.VMEM((2, BLOCK_A, 128), F32),
            pltpu.VMEM((BLOCK_A, 128), BF16),
            pltpu.VMEM((BLOCK_A, 128), BF16),
        ]
        + [sem] * 12
        + [sem((CHUNKS,))] * 8
        + [sem((2,)), sem],
        compiler_params=pltpu.CompilerParams(
            collective_id=0, has_side_effects=True, vmem_limit_bytes=60 * 2**20
        ),
        name="relay",
    )(pixels_first, kernels.reshape(TAPS * channels, inner))
    out = out.reshape(SIDE, SIDE, images, channels).transpose(2, 0, 1, 3)
    return out[None], (grads * scale).reshape(kernels.shape)


def solution(mesh):
    return jax.shard_map(
        body,
        mesh=mesh,
        in_specs=(
            P("section", "narrow", None, None, "wide"),
            P("section", None, None, "wide", "narrow"),
        ),
        out_specs=(
            P("section", "narrow", None, None, "wide"),
            P("section", None, None, "wide", "narrow"),
        ),
        check_vma=False,
    )
```

time: 493 us -> 84.2 us (0.17); the launches traced: 484 us -> 84 us
  waiting for transfers between devices: 233 us -> 0 us
  blocking collectives: 199 us -> 0 us
  Pallas kernels: 0 us -> 78.3 us
  matrix products: 20.6 us -> 0 us
  between operations: 14.8 us -> 0.64 us
  other arithmetic: 13.4 us -> 1.55 us
    psum x1 -> x0, waiting for transfers between devices: 230 us -> none  [body(): summed = lax.psum(spatial_conv(gathered, forward_kernel, 'HWIO'), 'wide')]
    unnamed x1 -> x0, blocking collectives: 141 us -> none
    pallas_call x0 -> x1, Pallas kernels: none -> 78.3 us  [body(): pl.pallas_call(kernel, out_shape=(jax.ShapeDtypeStruct((PIXELS, channels)...]
    all_gather x1 -> x0, blocking collectives: 57.1 us -> none  [body(): gathered = lax.all_gather(section_input[0], 'narrow', axis=0, tiled=True)]
    conv_general_dilated x3 -> x0, matrix products: 20.6 us -> none  [the longest x2 13.8 us: spatial_conv(): lax.conv_general_dilated(values, kernel, (1, 1), ((1, 1), (1, 1)), dimens...]
    convert_element_type x2 -> x0, other arithmetic: 7.91 us -> none  [the longest x1 4.25 us: body(): jnp.where(first_section, incoming * smooth_slope(summed), incoming)]
  transfers between devices with their start and end apart: 2 -> 0, of which waited for: 2 -> 0; matrix products, arithmetic and copies ran while one was open for 0% -> 0% of each run, Pallas kernels for 0% -> 0%
where the time goes in v2:
time: 84.2 us; the launch traced here: 84 us
  Pallas kernels  78.3 us (93%)
  local copies, waits for them, and re-layouts  3.51 us (4%)
  other arithmetic  1.55 us (2%)
    pallas_call x1, Pallas kernels, body(): pl.pallas_call(kernel, out_shape=(jax.ShapeDtypeStruct((PIXELS, channels)...  78.3 us
    reshape x1, local copies, waits for them, and re-layouts, body(): section_input[0].transpose(1, 2, 0, 3).reshape(PIXELS, channels)  1.8 us
    reshape x1, local copies, waits for them, and re-layouts, body(): out = out.reshape(SIDE, SIDE, images, channels).transpose(2, 0, 1, 3)  1.71 us

profile of v2, /device:TPU:2, one launch (start us, length us, event | category | flops | bytes accessed | tf_op | source)
XLA Modules:
  0.0 84.0 jit_solution(18277451901991545912)
XLA Ops:
  0.6 1.8 %reshape.16.x_ref = bf16[392,160]{1,0:T(8,128)(2,1)} reshape(bf16[14,14,2,160]{3,2,1,0:T(2,128)(2,1)} %bitcast.10) | data formatting | bytes 250880 | tf_op jit(solution)/shard_map/reshape | solution.py:421
  2.4 78.3 %relay.1 = (bf16[392,160]{1,0:T(8,128)(2,1)}, f32[1440,320]{1,0:T(8,128)S(1)}) custom-call(bf16[392,160]{1,0:T(8,128)(2,1)} %reshape.16.x_ref, bf16[1440,320]{1,0:T(8,128)(2,1)} %bitcast.9), custom_call_target="tpu_custom_call" | custom-call | tf_op jit(solution)/shard_map/relay/pallas_call | solution.py:422
  80.8 1.7 %reshape.18 = bf16[14,14,2,160]{3,2,1,0:T(2,128)(2,1)} reshape(bf16[392,160]{1,0:T(8,128)(2,1)} %get-tuple-element.4) | data formatting | bytes 250880 | tf_op jit(solution)/shard_map/reshape | solution.py:465
  82.5 1.5 %broadcast_multiply_fusion = f32[1440,320]{1,0:T(8,128)} fusion(f32[1440,320]{1,0:T(8,128)S(1)} %get-tuple-element.5), kind=kLoop, calls=%fused_computation | loop fusion | flops 460800 | bytes 3686400 | tf_op jit(solution)/shard_map/mul | solution.py:466

commit v3 on v2

--- a/solution.py
+++ b/solution.py
@@ -27,19 +27,13 @@
 SLOT = {(0, 0): 0, (0, 1): 1, (0, 2): 2, (1, 0): 3, (1, 1): 4, (1, 2): 5, (1, 3): 6, (0, 3): 7}
 FROM_PAIR = SLOT[(1, 0)]
 
-PLAN = (
-    (0, 1, "next_conv"),
-    (1, 0, "join"),
-    (5, 0, "spread_y"),
-    (3, 0, "sum_z"),
-    (6, 0, "forward_y"),
-    (2, 0, "sum_y"),
-    (7, 1, "second_conv"),
-    (3, 0, "meet"),
-    (9, 1, "kernel_grad"),
+SCHEDULE = (
+    "A1", "J0", "A2", "R0", "J1", "A3", "Y0", "J2", "A7", "Y1", "J3", "A4", "Z0", "Y2", "A5", "M0", "A6",
+    "Z1", "Y3", "J4", "Z2", "M1", "J5", "M2", "J6", "Y4", "Z3", "P1", "Y5", "P2", "Y6", "M3", "J7", "P0",
+    "Z4", "M4", "Z5", "F2", "M5", "Z6", "F1", "P3", "M6", "Y7", "P4", "P5", "C1", "P6", "Z7", "F4", "M7",
+    "F5", "F3", "F0", "C2", "F6", "G1", "C4", "P7", "C5", "C6", "G6", "F7", "C3", "G5", "G4", "X0", "G2",
+    "C7", "C0", "G0", "G7", "G3", "W0",
 )
-LAST = 7
-LATE_GRADS = (6, 7, 0)
 
 
 def chunk_dz(k):
@@ -101,12 +95,12 @@
     ex_in,
     act,
     act_all,
-    products,
     share,
     got_x,
     own_sum,
     pair_out,
     pair_in,
+    turned,
     s_load,
     s_img,
     s_relay,
@@ -162,18 +156,7 @@
     load = pltpu.make_async_copy(k_hbm, k_ref, s_load)
     load.start()
 
-    sign = 1 - 2 * section
     lane = lax.broadcasted_iota(jnp.int32, (1, LANES), 1)
-    pixel = lane // 2
-    row = pixel // SIDE
-    column = pixel - SIDE * row
-    for tap in range(TAPS):
-        there_row = row + sign * (tap // 3 - 1)
-        there_column = column + sign * (tap % 3 - 1)
-        inside = (there_row >= 0) & (there_row < SIDE) & (there_column >= 0) & (there_column < SIDE)
-        inside = (inside & (lane < PIXELS)).astype(F32)
-        masks_f[tap] = inside
-        masks[tap] = inside.astype(BF16)
     keep = (lane[:, :128] < SPILL).astype(BF16)
 
     def shift_of(tap, direction):
@@ -184,7 +167,6 @@
     own_f = jnp.concatenate([x_ref[...].astype(F32), blank], axis=0).T
     own = own_f.astype(BF16)
     images[0] = pack(own_f).astype(BF16)
-    grad_ref[...] = jnp.zeros_like(grad_ref)
 
     def image_copy(slot, dz, j):
         there = SLOT[(dz, (4 - j) % 4)]
@@ -233,7 +215,7 @@
         copy(buffer, buffer, send, r_pair, other).wait_send()
 
     def first_conv(k):
-        image = own if isinstance(k, int) else unpack(images[k], ROWS_A, keep)
+        image = own if k == 0 else unpack(images[k], ROWS_A, keep)
         for tap in range(TAPS):
             moved = image
             if tap != 4:
@@ -254,8 +236,7 @@
             near_copy(k, half).start()
 
     def next_conv(k):
-        @pl.when(k != FROM_PAIR)
-        def _():
+        if k != FROM_PAIR:
             arrived(images.at[k], r_img.at[k])
 
         first_conv(k)
@@ -313,30 +294,27 @@
         for block in range(4):
             piece = unpack(act[k, block].reshape(BLOCK_B, 128), 80, keep)
             act_all[k, pl.ds(80 * block, 80), :] = piece
-        products[...] = jnp.dot(k_ref[...], act_all[k], preferred_element_type=F32)
-        total = products[pl.ds(ROWS_A * 4, ROWS_A), :]
-        for tap in range(TAPS):
-            if tap != 4:
-                moved = pltpu.roll(products[pl.ds(ROWS_A * tap, ROWS_A), :], shift_of(tap, -sign), 1)
-                total = total + moved * masks_f[8 - tap]
+        total = None
+        for line in (1, 0, 2):
+            rows = pl.ds(3 * ROWS_A * line, 3 * ROWS_A)
+            product = jnp.dot(k_ref[rows], act_all[k], preferred_element_type=F32)
+            for place in range(3):
+                tap = 3 * line + place
+                moved = product[ROWS_A * place : ROWS_A * place + ROWS_A]
+                if tap != 4:
+                    moved = pltpu.roll(moved, shift_of(tap, -sign), 1) * masks_f[8 - tap]
+                total = moved if total is None else total + moved
         block = pack(total)
-        if isinstance(k, int):
-            own_sum[0] = block
-            return
-        dx = chunk_dx(k)
-
-        @pl.when(dx == 0)
-        def _():
-            own_sum[chunk_dz(k)] = block
-
-        @pl.when(dx != 0)
-        def _():
+        dz, dx = chunk_dz(k), chunk_dx(k)
+        if dx == 0:
+            own_sum[dz] = block
+        else:
             share[k] = block.astype(BF16)
             share_copy(k).start()
 
     def kernel_grad(k):
-        grad_ref[...] += lax.dot_general(
-            taps[k], act_all[k], (((1,), (1,)), ((), ())), preferred_element_type=F32
+        turned[...] += lax.dot_general(
+            act_all[k], taps[k], (((1,), (1,)), ((), ())), preferred_element_type=F32
         )
 
     def sum_x(dz):
@@ -346,60 +324,64 @@
             total = total + got_x[dz, j].astype(F32)
         return total
 
+    def pass_image(k):
+        arrived(images.at[FROM_PAIR], r_img.at[FROM_PAIR])
+        for j in (3, 2, 1):
+            image_copy(FROM_PAIR, 1, j).start()
+
+    across = copy(pair_out, pair_in, s_pair, r_pair, pair)
+
+    def send_across(k):
+        pair_out[...] = sum_x(1).astype(BF16)
+        across.start()
+
+    def finish(k):
+        total = sum_x(0)
+        across.wait_recv()
+        total = total + pair_in[...].astype(F32)
+        out_ref[...] = unpack(total, ROWS_A, keep.astype(F32)).T[:PIXELS].astype(BF16)
+
     stages = dict(
-        next_conv=next_conv,
-        join=join,
-        sum_y=sum_y,
-        sum_z=sum_z,
-        meet=meet,
-        spread_y=spread_y,
-        forward_y=forward_y,
-        second_conv=second_conv,
-        kernel_grad=kernel_grad,
+        A=next_conv,
+        J=join,
+        Y=sum_y,
+        Z=sum_z,
+        M=meet,
+        P=spread_y,
+        F=forward_y,
+        C=second_conv,
+        G=kernel_grad,
+        R=pass_image,
+        X=send_across,
+        W=finish,
     )
 
-    def step(t, carry):
-        for when, j in ((1, 2), (5, 1)):
-
-            @pl.when(t == when)
-            def _():
-                image_copy(0, 0, j).start()
-
-        @pl.when(t == FROM_PAIR)
-        def _():
-            arrived(images.at[FROM_PAIR], r_img.at[FROM_PAIR])
-            for j in (3, 2, 1):
-                image_copy(FROM_PAIR, 1, j).start()
-
-        for lag, first, stage in PLAN:
-
-            @pl.when((t >= lag + first) & (t < CHUNKS + lag))
-            def _():
-                stages[stage](t - lag)
-
-        return carry
-
+    pl.semaphore_wait(barrier, len(peers))
+    to_pair.start()
+    image_copy(0, 0, 3).start()
+    sign = 1 - 2 * section
+    pixel = lane // 2
+    row = pixel // SIDE
+    column = pixel - SIDE * row
+    for tap in range(TAPS):
+        there_row = row + sign * (tap // 3 - 1)
+        there_column = column + sign * (tap % 3 - 1)
+        inside = (there_row >= 0) & (there_row < SIDE) & (there_column >= 0) & (there_column < SIDE)
+        inside = (inside & (lane < PIXELS)).astype(F32)
+        masks_f[tap] = inside
+        masks[tap] = inside.astype(BF16)
     load.wait()
     flipped[...] = k_ref[...].T
     first_conv(0)
-    pl.semaphore_wait(barrier, len(peers))
-    to_pair.start()
-    image_copy(0, 0, 3).start()
     send_parts(0)
-
-    lax.fori_loop(1, CHUNKS + LAST, step, 0)
-
-    across = copy(pair_out, pair_in, s_pair, r_pair, pair)
-    pair_out[...] = sum_x(1).astype(BF16)
-    across.start()
-    second_conv(0)
-    for k in LATE_GRADS:
-        kernel_grad(k)
-    total = sum_x(0)
-    across.wait_recv()
-    total = total + pair_in[...].astype(F32)
-    out_ref[...] = unpack(total, ROWS_A, keep.astype(F32)).T[:PIXELS].astype(BF16)
-
+    image_copy(0, 0, 2).start()
+    image_copy(0, 0, 1).start()
+    turned[...] = jnp.zeros_like(turned)
+
+    for stage, k in SCHEDULE:
+        stages[stage](int(k))
+
+    grad_ref[...] = turned[...].T
     across.wait_send()
     left(images.at[pl.ds(0, 7)], s_img)
     left(relayed, s_relay)
@@ -447,12 +429,12 @@
             pltpu.VMEM((CHUNKS, QUARTER, 128), BF16),
             pltpu.VMEM((CHUNKS, 4, 4, QUARTER, 128), BF16),
             pltpu.VMEM((CHUNKS, inner, LANES), BF16),
-            pltpu.VMEM((TAPS * channels, LANES), F32),
             pltpu.VMEM((CHUNKS, BLOCK_A, 128), BF16),
             pltpu.VMEM((2, 3, BLOCK_A, 128), BF16),
             pltpu.VMEM((2, BLOCK_A, 128), F32),
             pltpu.VMEM((BLOCK_A, 128), BF16),
             pltpu.VMEM((BLOCK_A, 128), BF16),
+            pltpu.VMEM((inner, TAPS * channels), F32),
         ]
         + [sem] * 12
         + [sem((CHUNKS,))] * 8

time: 84.2 us -> 78.1 us (0.928)
  Pallas kernels: 78.3 us -> 72.3 us
    pallas_call x1, Pallas kernels: 78.3 us -> 72.3 us  [body(): pl.pallas_call(kernel, out_shape=(jax.ShapeDtypeStruct((PIXELS, channels)...]
where the time goes in v3:
time: 78.1 us; the launch traced here: 78 us
  Pallas kernels  72.3 us (93%)
  local copies, waits for them, and re-layouts  3.51 us (4%)
  other arithmetic  1.55 us (2%)
    pallas_call x1, Pallas kernels, body(): pl.pallas_call(kernel, out_shape=(jax.ShapeDtypeStruct((PIXELS, channels)...  72.3 us
    reshape x1, local copies, waits for them, and re-layouts, body(): section_input[0].transpose(1, 2, 0, 3).reshape(PIXELS, channels)  1.8 us
    reshape x1, local copies, waits for them, and re-layouts, body(): out = out.reshape(SIDE, SIDE, images, channels).transpose(2, 0, 1, 3)  1.71 us

profile of v3, /device:TPU:2, one launch (start us, length us, event | category | flops | bytes accessed | tf_op | source)
XLA Modules:
  0.0 78.0 jit_solution(12522634811877666905)
XLA Ops:
  0.6 1.8 %reshape.16.x_ref = bf16[392,160]{1,0:T(8,128)(2,1)} reshape(bf16[14,14,2,160]{3,2,1,0:T(2,128)(2,1)} %bitcast.10) | data formatting | bytes 250880 | tf_op jit(solution)/shard_map/reshape | solution.py:403
  2.4 72.3 %relay.1 = (bf16[392,160]{1,0:T(8,128)(2,1)}, f32[1440,320]{1,0:T(8,128)S(1)}) custom-call(bf16[392,160]{1,0:T(8,128)(2,1)} %reshape.16.x_ref, bf16[1440,320]{1,0:T(8,128)(2,1)} %bitcast.9), custom_call_target="tpu_custom_call" | custom-call | tf_op jit(solution)/shard_map/relay/pallas_call | solution.py:404
  74.7 1.7 %reshape.18 = bf16[14,14,2,160]{3,2,1,0:T(2,128)(2,1)} reshape(bf16[392,160]{1,0:T(8,128)(2,1)} %get-tuple-element.4) | data formatting | bytes 250880 | tf_op jit(solution)/shard_map/reshape | solution.py:447
  76.4 1.5 %broadcast_multiply_fusion = f32[1440,320]{1,0:T(8,128)} fusion(f32[1440,320]{1,0:T(8,128)S(1)} %get-tuple-element.5), kind=kLoop, calls=%fused_computation | loop fusion | flops 460800 | bytes 3686400 | tf_op jit(solution)/shard_map/mul | solution.py:448

commit v4 on v3

--- a/solution.py
+++ b/solution.py
@@ -1,3 +1,4 @@
+import functools
 import math
 
 import jax
@@ -27,12 +28,14 @@
 SLOT = {(0, 0): 0, (0, 1): 1, (0, 2): 2, (1, 0): 3, (1, 1): 4, (1, 2): 5, (1, 3): 6, (0, 3): 7}
 FROM_PAIR = SLOT[(1, 0)]
 
+STRAIGHT_SUMS = (0, 1, 3)
+STRAIGHT_GATHERS = (5, 6, 7)
+
 SCHEDULE = (
-    "A1", "J0", "A2", "R0", "J1", "A3", "Y0", "J2", "A7", "Y1", "J3", "A4", "Z0", "Y2", "A5", "M0", "A6",
-    "Z1", "Y3", "J4", "Z2", "M1", "J5", "M2", "J6", "Y4", "Z3", "P1", "Y5", "P2", "Y6", "M3", "J7", "P0",
-    "Z4", "M4", "Z5", "F2", "M5", "Z6", "F1", "P3", "M6", "Y7", "P4", "P5", "C1", "P6", "Z7", "F4", "M7",
-    "F5", "F3", "F0", "C2", "F6", "G1", "C4", "P7", "C5", "C6", "G6", "F7", "C3", "G5", "G4", "X0", "G2",
-    "C7", "C0", "G0", "G7", "G3", "W0",
+    "A1", "R0", "A3", "Y0", "A7", "Y1", "A4", "A5", "Y3", "A6", "Z1", "Z0", "M1", "J4", "J7", "M0", "J5",
+    "Z3", "A2", "M3", "J6", "Y4", "P1", "Y5", "J2", "Y6", "P3", "Y7", "Z4", "M4", "Z5", "F1", "P0", "M5",
+    "Y2", "Z6", "F3", "M6", "P4", "Z7", "M7", "P5", "Z2", "M2", "F4", "P6", "C3", "G3", "C5", "P2", "P7",
+    "F0", "C4", "C6", "G4", "F2", "G5", "C1", "C7", "X0", "C2", "G1", "G7", "C0", "G2", "G0", "G6", "W0",
 )
 
 
@@ -72,6 +75,7 @@
 
 
 def kernel(
+    scale,
     x_ref,
     k_hbm,
     out_ref,
@@ -112,6 +116,8 @@
     s_ay,
     s_af,
     s_share,
+    s_straight,
+    s_gather,
     s_pair,
     r_img,
     r_relay,
@@ -148,7 +154,7 @@
         )
 
     barrier = pltpu.get_barrier_semaphore()
-    peers = [at_y(j) for j in (1, 3)] + [at_z(j) for j in (1, 2, 3)]
+    peers = [at_y(j) for j in (1, 2, 3)] + [at_z(j) for j in (1, 2, 3)]
     peers += [at_x(j) for j in (1, 2, 3)] + [pair, other]
     for peer in peers:
         pl.semaphore_signal(barrier, inc=1, device_id=peer, device_id_type=MESH)
@@ -164,7 +170,7 @@
         return (LANES - direction * offset) % LANES
 
     blank = jnp.zeros((LANES - PIXELS, ROWS_A), F32)
-    own_f = jnp.concatenate([x_ref[...].astype(F32), blank], axis=0).T
+    own_f = jnp.concatenate([x_ref[...].reshape(PIXELS, ROWS_A).astype(F32), blank], axis=0).T
     own = own_f.astype(BF16)
     images[0] = pack(own_f).astype(BF16)
 
@@ -182,6 +188,13 @@
     def near_copy(k, half):
         j = 3 - 2 * half
         return copy(part.at[k, (y + j) % 4, half], got_y.at[k, 0, half], s_near, r_y.at[k], at_y(j))
+
+    def straight_copy(k, j):
+        return copy(part.at[k, (y + j) % 4], got_y.at[k, j - 1], s_straight, r_y.at[k], at_y(j))
+
+    def gather_copy(k, j):
+        here = act.at[k, y]
+        return copy(here, here, s_gather, r_ay.at[k], at_y(j))
 
     def join_copy(k, half):
         return copy(joined.at[k, half], got_y.at[k, 1, half], s_join, r_y.at[k], at_y(1 + 2 * half))
@@ -230,6 +243,10 @@
                 part[k, block, half] = rows.astype(BF16)
 
     def send_parts(k):
+        if k in STRAIGHT_SUMS:
+            for j in (2, 1, 3):
+                straight_copy(k, j).start()
+            return
         for half in range(2):
             relay_copy(k, half).start()
         for half in range(2):
@@ -250,10 +267,11 @@
             join_copy(k, half).start()
 
     def sum_y(k):
-        arrived(got_y.at[k], r_y.at[k])
+        pieces = 3 if k in STRAIGHT_SUMS else 2
+        arrived(got_y.at[k, pl.ds(0, pieces)], r_y.at[k])
         for half in range(2):
             total = part_f[k, y, half]
-            for j in range(2):
+            for j in range(pieces):
                 total = total + got_y[k, j, half].astype(F32)
             for side in range(2):
                 piece = total[QUARTER * side : QUARTER * side + QUARTER]
@@ -281,6 +299,10 @@
 
     def spread_y(k):
         arrived(got_z.at[k], r_az.at[k])
+        if k in STRAIGHT_GATHERS:
+            for j in (2, 1, 3):
+                gather_copy(k, j).start()
+            return
         for side in range(2):
             ay_copy(k, side).start()
 
@@ -290,7 +312,10 @@
             af_copy(k, side).start()
 
     def second_conv(k):
-        arrived(act.at[k, 0], r_af.at[k])
+        if k in STRAIGHT_GATHERS:
+            arrived(act.at[k, pl.ds(0, 3)], r_ay.at[k])
+        else:
+            arrived(act.at[k, 0], r_af.at[k])
         for block in range(4):
             piece = unpack(act[k, block].reshape(BLOCK_B, 128), 80, keep)
             act_all[k, pl.ds(80 * block, 80), :] = piece
@@ -336,10 +361,12 @@
         across.start()
 
     def finish(k):
+        grad_ref[...] = turned[...].T * scale
         total = sum_x(0)
         across.wait_recv()
         total = total + pair_in[...].astype(F32)
-        out_ref[...] = unpack(total, ROWS_A, keep.astype(F32)).T[:PIXELS].astype(BF16)
+        total = unpack(total, ROWS_A, keep.astype(F32)).T[:PIXELS].astype(BF16)
+        out_ref[...] = total.reshape(out_ref.shape)
 
     stages = dict(
         A=next_conv,
@@ -381,17 +408,21 @@
     for stage, k in SCHEDULE:
         stages[stage](int(k))
 
-    grad_ref[...] = turned[...].T
     across.wait_send()
     left(images.at[pl.ds(0, 7)], s_img)
-    left(relayed, s_relay)
-    left(relayed, s_near)
-    left(relayed, s_join)
+    round_sums = CHUNKS - len(STRAIGHT_SUMS)
+    round_gathers = CHUNKS - len(STRAIGHT_GATHERS)
+    for send in (s_relay, s_near, s_join):
+        left(relayed.at[pl.ds(0, round_sums)], send)
+    left(act.at[pl.ds(0, round_gathers), pl.ds(0, 2)], s_ay)
+    left(act.at[pl.ds(0, round_gathers), 0], s_af)
+    if STRAIGHT_SUMS:
+        left(got_y.at[pl.ds(0, len(STRAIGHT_SUMS))], s_straight)
+    if STRAIGHT_GATHERS:
+        left(act.at[pl.ds(0, len(STRAIGHT_GATHERS)), pl.ds(0, 3)], s_gather)
     left(got_z, s_z)
     left(ex_out, s_ex)
     left(got_z, s_az)
-    left(act.at[:, pl.ds(0, 2)], s_ay)
-    left(act.at[:, 0], s_af)
     left(share.at[pl.ds(0, 6)], s_share)
 
 
@@ -400,11 +431,11 @@
     inner = kernels.shape[4]
     scale = 1.0 / math.sqrt(CHUNKS * images * SIDE * SIDE)
     sem = pltpu.SemaphoreType.DMA
-    pixels_first = section_input[0].transpose(1, 2, 0, 3).reshape(PIXELS, channels)
+    pixels_first = section_input[0].transpose(1, 2, 0, 3).reshape(SIDE * SIDE, images, channels)
     out, grads = pl.pallas_call(
-        kernel,
+        functools.partial(kernel, scale),
         out_shape=(
-            jax.ShapeDtypeStruct((PIXELS, channels), BF16),
+            jax.ShapeDtypeStruct((SIDE * SIDE, images, channels), BF16),
             pltpu.VMEM((TAPS * channels, inner), F32),
         ),
         in_specs=[pl.BlockSpec(memory_space=pltpu.VMEM), pl.BlockSpec(memory_space=pl.ANY)],
@@ -420,7 +451,7 @@
             pltpu.VMEM((CHUNKS, 4, 2, HALF, 128), F32),
             pltpu.VMEM((CHUNKS, 2, HALF, 128), BF16),
             pltpu.VMEM((CHUNKS, 2, HALF, 128), BF16),
-            pltpu.VMEM((CHUNKS, 2, 2, HALF, 128), BF16),
+            pltpu.VMEM((CHUNKS, 3, 2, HALF, 128), BF16),
             pltpu.VMEM((CHUNKS, 4, QUARTER, 128), BF16),
             pltpu.VMEM((CHUNKS, 4, QUARTER, 128), F32),
             pltpu.VMEM((CHUNKS, 3, QUARTER, 128), BF16),
@@ -436,7 +467,7 @@
             pltpu.VMEM((BLOCK_A, 128), BF16),
             pltpu.VMEM((inner, TAPS * channels), F32),
         ]
-        + [sem] * 12
+        + [sem] * 14
         + [sem((CHUNKS,))] * 8
         + [sem((2,)), sem],
         compiler_params=pltpu.CompilerParams(
@@ -445,7 +476,7 @@
         name="relay",
     )(pixels_first, kernels.reshape(TAPS * channels, inner))
     out = out.reshape(SIDE, SIDE, images, channels).transpose(2, 0, 1, 3)
-    return out[None], (grads * scale).reshape(kernels.shape)
+    return out[None], grads.reshape(kernels.shape)
 
 
 def solution(mesh):

time: 78.1 us -> 71.1 us (0.910)
  Pallas kernels: 72.3 us -> 68.3 us
  other arithmetic: 1.55 us -> 0 us
  local copies, waits for them, and re-layouts: 3.51 us -> 2.04 us
    pallas_call x1, Pallas kernels: 72.3 us -> 68.3 us  [body(): pl.pallas_call(functools.partial(kernel, scale), out_shape=(jax.ShapeDtyp...]
    reshape x2 -> x0, local copies, waits for them, and re-layouts: 3.51 us -> none  [the longest x1 1.8 us: body(): section_input[0].transpose(1, 2, 0, 3).reshape(PIXELS, channels)]
    unnamed x0 -> x4, local copies, waits for them, and re-layouts: none -> 2.04 us
    mul x1 -> x0, other arithmetic: 1.55 us -> none  [body(): return (out[None], (grads * scale).reshape(kernels.shape))]
where the time goes in v4:
time: 71.1 us; the launch traced here: 71 us
  Pallas kernels  68.3 us (96%)
  local copies, waits for them, and re-layouts  2.04 us (3%)
    pallas_call x1, Pallas kernels, body(): pl.pallas_call(functools.partial(kernel, scale), out_shape=(jax.ShapeDtyp...  68.3 us
    unnamed x4, local copies, waits for them, and re-layouts  2.04 us

profile of v4, /device:TPU:2, one launch (start us, length us, event | category | flops | bytes accessed | tf_op | source)
XLA Modules:
  0.0 71.0 jit_solution(15644039042682498159)
XLA Ops:
  0.6 68.3 %relay.1 = (bf16[196,2,160]{2,1,0:T(2,128)(2,1)}, f32[1440,320]{1,0:T(8,128)S(1)}) custom-call(bf16[196,2,160]{2,1,0:T(2,128)(2,1)} %bitcast.14, bf16[1440,320]{1,0:T(8,128)(2,1)} %bitcast.13), custom_call_target="tpu_custom_call" | custom-call | tf_op jit(solution)/shard_map/relay/pallas_call | solution.py:435
  68.9 0.0 copy-start
  68.9 1.4 %copy.6 = f32[1,3,3,160,320]{4,3,2,1,0:T(8,128)} copy(f32[1,3,3,160,320]{4,3,2,1,0:T(8,128)S(1)} %bitcast.12) | data formatting | bytes 3686400
  70.3 0.0 copy-done
  70.3 0.7 copy.7
Async XLA Ops:
  68.9 1.4 %copy-start = (bf16[196,2,160]{2,1,0:T(2,128)(2,1)S(1)}, bf16[196,2,160]{2,1,0:T(2,128)(2,1)}, u32[]{:S(2)}) copy-start(bf16[196,2,160]{2,1,0:T(2,128)(2,1)} %get-tuple-element.4) | copy-start | bytes 376324

commit v5 on v4

--- a/solution.py
+++ b/solution.py
@@ -28,14 +28,14 @@
 SLOT = {(0, 0): 0, (0, 1): 1, (0, 2): 2, (1, 0): 3, (1, 1): 4, (1, 2): 5, (1, 3): 6, (0, 3): 7}
 FROM_PAIR = SLOT[(1, 0)]
 
-STRAIGHT_SUMS = (0, 1, 3)
-STRAIGHT_GATHERS = (5, 6, 7)
+STRAIGHT_SUMS = (0, 1, 3, 4)
+STRAIGHT_GATHERS = (4, 5, 6, 7)
 
 SCHEDULE = (
-    "A1", "R0", "A3", "Y0", "A7", "Y1", "A4", "A5", "Y3", "A6", "Z1", "Z0", "M1", "J4", "J7", "M0", "J5",
-    "Z3", "A2", "M3", "J6", "Y4", "P1", "Y5", "J2", "Y6", "P3", "Y7", "Z4", "M4", "Z5", "F1", "P0", "M5",
-    "Y2", "Z6", "F3", "M6", "P4", "Z7", "M7", "P5", "Z2", "M2", "F4", "P6", "C3", "G3", "C5", "P2", "P7",
-    "F0", "C4", "C6", "G4", "F2", "G5", "C1", "C7", "X0", "C2", "G1", "G7", "C0", "G2", "G0", "G6", "W0",
+    "A1", "R0", "R1", "A3", "Y0", "A4", "Y1", "A6", "Z0", "Y3", "A5", "M0", "A2", "Z1", "Y4", "M1", "J6",
+    "A7", "J5", "Z3", "M3", "P0", "Z4", "J2", "Y6", "M4", "J7", "P1", "Y5", "P3", "Y2", "Z6", "M6", "P4",
+    "Y7", "Z5", "Z2", "M5", "F3", "F1", "M2", "P6", "Z7", "C4", "P5", "M7", "C1", "P2", "G4", "C6", "P7",
+    "C5", "F0", "G5", "F2", "C3", "G3", "C7", "X0", "G7", "C2", "C0", "G2", "G0", "G1", "G6", "W0",
 )
 
 
@@ -76,10 +76,11 @@
 
 def kernel(
     scale,
-    x_ref,
+    x_hbm,
     k_hbm,
     out_ref,
     grad_ref,
+    x_ref,
     k_ref,
     masks,
     masks_f,
@@ -105,6 +106,7 @@
     pair_out,
     pair_in,
     turned,
+    s_load_x,
     s_load,
     s_img,
     s_relay,
@@ -119,6 +121,7 @@
     s_straight,
     s_gather,
     s_pair,
+    r_pair_img,
     r_img,
     r_relay,
     r_y,
@@ -154,11 +157,13 @@
         )
 
     barrier = pltpu.get_barrier_semaphore()
-    peers = [at_y(j) for j in (1, 2, 3)] + [at_z(j) for j in (1, 2, 3)]
-    peers += [at_x(j) for j in (1, 2, 3)] + [pair, other]
+    peers = [pair] + [at_z(j) for j in (2, 1, 3)] + [at_x(j) for j in (2, 1, 3)]
+    peers += [at_y(j) for j in (2, 1, 3)] + [other]
     for peer in peers:
         pl.semaphore_signal(barrier, inc=1, device_id=peer, device_id_type=MESH)
 
+    load_x = pltpu.make_async_copy(x_hbm, x_ref, s_load_x)
+    load_x.start()
     load = pltpu.make_async_copy(k_hbm, k_ref, s_load)
     load.start()
 
@@ -170,15 +175,26 @@
         return (LANES - direction * offset) % LANES
 
     blank = jnp.zeros((LANES - PIXELS, ROWS_A), F32)
+    load_x.wait()
     own_f = jnp.concatenate([x_ref[...].reshape(PIXELS, ROWS_A).astype(F32), blank], axis=0).T
     own = own_f.astype(BF16)
     images[0] = pack(own_f).astype(BF16)
 
-    def image_copy(slot, dz, j):
-        there = SLOT[(dz, (4 - j) % 4)]
-        return copy(images.at[slot], images.at[there], s_img, r_img.at[there], at_x(j))
-
-    to_pair = copy(images.at[0], images.at[FROM_PAIR], s_img, r_img.at[FROM_PAIR], pair)
+    def image_copy(j):
+        there = SLOT[(0, (4 - j) % 4)]
+        return copy(images.at[0], images.at[there], s_img, r_img.at[there], at_x(j))
+
+    pieces_of_image = (pl.ds(0, 256), pl.ds(256, BLOCK_A - 256))
+
+    def pair_copy(piece):
+        rows = pieces_of_image[piece]
+        there = images.at[FROM_PAIR, rows]
+        return copy(images.at[0, rows], there, s_img, r_pair_img.at[piece], pair)
+
+    def pass_copy(piece, j):
+        rows = pieces_of_image[piece]
+        slot = SLOT[(1, (4 - j) % 4)]
+        return copy(images.at[FROM_PAIR, rows], images.at[slot, rows], s_img, r_img.at[slot], at_x(j))
 
     def relay_copy(k, half):
         return copy(
@@ -349,10 +365,10 @@
             total = total + got_x[dz, j].astype(F32)
         return total
 
-    def pass_image(k):
-        arrived(images.at[FROM_PAIR], r_img.at[FROM_PAIR])
+    def pass_image(piece):
+        arrived(images.at[FROM_PAIR, pieces_of_image[piece]], r_pair_img.at[piece])
         for j in (3, 2, 1):
-            image_copy(FROM_PAIR, 1, j).start()
+            pass_copy(piece, j).start()
 
     across = copy(pair_out, pair_in, s_pair, r_pair, pair)
 
@@ -384,8 +400,9 @@
     )
 
     pl.semaphore_wait(barrier, len(peers))
-    to_pair.start()
-    image_copy(0, 0, 3).start()
+    pair_copy(0).start()
+    pair_copy(1).start()
+    image_copy(3).start()
     sign = 1 - 2 * section
     pixel = lane // 2
     row = pixel // SIDE
@@ -401,8 +418,8 @@
     flipped[...] = k_ref[...].T
     first_conv(0)
     send_parts(0)
-    image_copy(0, 0, 2).start()
-    image_copy(0, 0, 1).start()
+    image_copy(2).start()
+    image_copy(1).start()
     turned[...] = jnp.zeros_like(turned)
 
     for stage, k in SCHEDULE:
@@ -438,9 +455,10 @@
             jax.ShapeDtypeStruct((SIDE * SIDE, images, channels), BF16),
             pltpu.VMEM((TAPS * channels, inner), F32),
         ),
-        in_specs=[pl.BlockSpec(memory_space=pltpu.VMEM), pl.BlockSpec(memory_space=pl.ANY)],
+        in_specs=[pl.BlockSpec(memory_space=pl.ANY)] * 2,
         out_specs=[pl.BlockSpec(memory_space=pltpu.VMEM)] * 2,
         scratch_shapes=[
+            pltpu.VMEM((SIDE * SIDE, images, channels), BF16),
             pltpu.VMEM((TAPS * channels, inner), BF16),
             pltpu.VMEM((TAPS, 1, LANES), BF16),
             pltpu.VMEM((TAPS, 1, LANES), F32),
@@ -467,7 +485,8 @@
             pltpu.VMEM((BLOCK_A, 128), BF16),
             pltpu.VMEM((inner, TAPS * channels), F32),
         ]
-        + [sem] * 14
+        + [sem] * 15
+        + [sem((2,))]
         + [sem((CHUNKS,))] * 8
         + [sem((2,)), sem],
         compiler_params=pltpu.CompilerParams(

time: 71.1 us -> 69.9 us (0.983)
  the two profiles are of different devices: /device:TPU:2 before, /device:TPU:6 now
where the time goes in v5:
time: 69.9 us; the launch traced here: 69.8 us
  Pallas kernels  67.1 us (96%)
  local copies, waits for them, and re-layouts  2.04 us (3%)
    pallas_call x1, Pallas kernels, body(): pl.pallas_call(functools.partial(kernel, scale), out_shape=(jax.ShapeDtyp...  67.1 us
    unnamed x4, local copies, waits for them, and re-layouts  2.04 us

profile of v5, /device:TPU:6, one launch (start us, length us, event | category | flops | bytes accessed | tf_op | source)
XLA Modules:
  0.0 69.8 jit_solution(17546493202576016587)
XLA Ops:
  0.6 67.1 %relay.1 = (bf16[196,2,160]{2,1,0:T(2,128)(2,1)}, f32[1440,320]{1,0:T(8,128)S(1)}) custom-call(bf16[196,2,160]{2,1,0:T(2,128)(2,1)} %bitcast.14, bf16[1440,320]{1,0:T(8,128)(2,1)} %bitcast.13), custom_call_target="tpu_custom_call" | custom-call | tf_op jit(solution)/shard_map/relay/pallas_call | solution.py:452
  67.8 0.0 copy-start
  67.8 1.4 %copy.6 = f32[1,3,3,160,320]{4,3,2,1,0:T(8,128)} copy(f32[1,3,3,160,320]{4,3,2,1,0:T(8,128)S(1)} %bitcast.12) | data formatting | bytes 3686400
  69.1 0.0 copy-done
  69.1 0.7 copy.7
Async XLA Ops:
  67.8 1.4 %copy-start = (bf16[196,2,160]{2,1,0:T(2,128)(2,1)S(1)}, bf16[196,2,160]{2,1,0:T(2,128)(2,1)}, u32[]{:S(2)}) copy-start(bf16[196,2,160]{2,1,0:T(2,128)(2,1)} %get-tuple-element.4) | copy-start | bytes 376324

commit v6 on v5

--- a/solution.py
+++ b/solution.py
@@ -34,8 +34,8 @@
 SCHEDULE = (
     "A1", "R0", "R1", "A3", "Y0", "A4", "Y1", "A6", "Z0", "Y3", "A5", "M0", "A2", "Z1", "Y4", "M1", "J6",
     "A7", "J5", "Z3", "M3", "P0", "Z4", "J2", "Y6", "M4", "J7", "P1", "Y5", "P3", "Y2", "Z6", "M6", "P4",
-    "Y7", "Z5", "Z2", "M5", "F3", "F1", "M2", "P6", "Z7", "C4", "P5", "M7", "C1", "P2", "G4", "C6", "P7",
-    "C5", "F0", "G5", "F2", "C3", "G3", "C7", "X0", "G7", "C2", "C0", "G2", "G0", "G1", "G6", "W0",
+    "Y7", "Z5", "Z2", "M5", "F3", "F1", "M2", "P6", "Z7", "C4", "P5", "M7", "C1", "G4", "C6", "P2", "P7",
+    "C3", "C5", "F0", "G5", "F2", "G3", "G1", "G6", "X0", "C7", "C2", "G7", "C0", "G2", "G0", "W0",
 )
 
 
@@ -452,7 +452,7 @@
     out, grads = pl.pallas_call(
         functools.partial(kernel, scale),
         out_shape=(
-            jax.ShapeDtypeStruct((SIDE * SIDE, images, channels), BF16),
+            pltpu.VMEM((SIDE * SIDE, images, channels), BF16),
             pltpu.VMEM((TAPS * channels, inner), F32),
         ),
         in_specs=[pl.BlockSpec(memory_space=pl.ANY)] * 2,

time: 69.9 us -> 69.1 us (0.989)
  the two profiles are of different devices: /device:TPU:6 before, /device:TPU:2 now
where the time goes in v6:
time: 69.1 us; the launch traced here: 68.8 us
  Pallas kernels  66.1 us (96%)
  local copies, waits for them, and re-layouts  2.04 us (3%)
    pallas_call x1, Pallas kernels, body(): pl.pallas_call(functools.partial(kernel, scale), out_shape=(pltpu.VMEM((S...  66.1 us
    unnamed x2, local copies, waits for them, and re-layouts  2.04 us

profile of v6, /device:TPU:2, one launch (start us, length us, event | category | flops | bytes accessed | tf_op | source)
XLA Modules:
  0.0 68.8 jit_solution(13883040540486125565)
XLA Ops:
  0.6 66.1 %relay.1 = (bf16[196,2,160]{2,1,0:T(2,128)(2,1)S(1)}, f32[1440,320]{1,0:T(8,128)S(1)}) custom-call(bf16[196,2,160]{2,1,0:T(2,128)(2,1)} %bitcast.15, bf16[1440,320]{1,0:T(8,128)(2,1)} %bitcast.14), custom_call_target="tpu_custom_call" | custom-call | tf_op jit(solution)/shard_map/relay/pallas_call | solution.py:452
  66.8 0.7 copy.6
  67.5 1.4 %copy.7 = f32[1,3,3,160,320]{4,3,2,1,0:T(8,128)} copy(f32[1,3,3,160,320]{4,3,2,1,0:T(8,128)S(1)} %bitcast.12) | data formatting | bytes 3686400

commit v7 on v6

--- a/solution.py
+++ b/solution.py
@@ -34,8 +34,8 @@
 SCHEDULE = (
     "A1", "R0", "R1", "A3", "Y0", "A4", "Y1", "A6", "Z0", "Y3", "A5", "M0", "A2", "Z1", "Y4", "M1", "J6",
     "A7", "J5", "Z3", "M3", "P0", "Z4", "J2", "Y6", "M4", "J7", "P1", "Y5", "P3", "Y2", "Z6", "M6", "P4",
-    "Y7", "Z5", "Z2", "M5", "F3", "F1", "M2", "P6", "Z7", "C4", "P5", "M7", "C1", "G4", "C6", "P2", "P7",
-    "C3", "C5", "F0", "G5", "F2", "G3", "G1", "G6", "X0", "C7", "C2", "G7", "C0", "G2", "G0", "W0",
+    "Y7", "Z5", "Z2", "M5", "F3", "F1", "M2", "P6", "Z7", "P5", "M7", "C4", "C1", "C6", "P2", "P7", "G4",
+    "C5", "F0", "C3", "F2", "G5", "G3", "G1", "G6", "X0", "C7", "C2", "G7", "C0", "G2", "G0", "W0",
 )
 
 

time: 69.1 us -> 69.8 us (1.010)
  no operation moved by 1% of the time
where the time goes in v7:
time: 69.8 us; the launch traced here: 68.9 us
  Pallas kernels  66.2 us (95%)
  local copies, waits for them, and re-layouts  2.04 us (3%)
    pallas_call x1, Pallas kernels, body(): pl.pallas_call(functools.partial(kernel, scale), out_shape=(pltpu.VMEM((S...  66.2 us
    unnamed x2, local copies, waits for them, and re-layouts  2.04 us

profile of v7, /device:TPU:2, one launch (start us, length us, event | category | flops | bytes accessed | tf_op | source)
XLA Modules:
  0.0 68.9 jit_solution(9020299697136959249)
XLA Ops:
  0.6 66.2 %relay.1 = (bf16[196,2,160]{2,1,0:T(2,128)(2,1)S(1)}, f32[1440,320]{1,0:T(8,128)S(1)}) custom-call(bf16[196,2,160]{2,1,0:T(2,128)(2,1)} %bitcast.15, bf16[1440,320]{1,0:T(8,128)(2,1)} %bitcast.14), custom_call_target="tpu_custom_call" | custom-call | tf_op jit(solution)/shard_map/relay/pallas_call | solution.py:452
  66.8 0.7 copy.6
  67.5 1.4 %copy.7 = f32[1,3,3,160,320]{4,3,2,1,0:T(8,128)} copy(f32[1,3,3,160,320]{4,3,2,1,0:T(8,128)S(1)} %bitcast.12) | data formatting | bytes 3686400
